TPU v7x, 512 devices: a whole 4x4x16 slice. The times are simulated.
512 devices in a mesh: row: 32 (over z_lo, x, core), col: 16 (over z_hi, y).
Axes of the slice: x: 4, y: 4, z: 16 (z_hi: 4, z_lo: 4; z = z_hi * 4 + z_lo), core: 2. Of those that a mesh axis runs over, the one named last changes fastest.
Arguments:
- acts_in: bfloat16 [1024, 8192], P('col', 'row'), may hold values from -72 to 72, as said below
- grad_hidden: bfloat16 [1024, 32768], P('row', 'col'), may hold values from -1.2 to 1.2, as said below
- acts_hidden: bfloat16 [1024, 32768], P('col', 'row'), may hold values from -72 to 72, as said below
- grad_out: bfloat16 [1024, 8192], P('row', 'col'), may hold values from -1.2 to 1.2, as said below
- row_state_up: float32 [8192], P('row'), may hold values from 0.01 to 1
- col_state_up: float32 [32768], P('col'), may hold values from 0.01 to 1
- row_state_down: float32 [32768], P('row'), may hold values from 0.01 to 1
- col_state_down: float32 [8192], P('col'), may hold values from 0.01 to 1
Outputs:
- update_up: bfloat16 [8192, 32768], P('row', 'col')
- row_new_up: float32 [8192], P('row')
- col_new_up: float32 [32768], P('col')
- update_down: bfloat16 [32768, 8192], P('row', 'col')
- row_new_down: float32 [32768], P('row')
- col_new_down: float32 [8192], P('col')
Inputs may be any that keep to these rules, and one draw needn't show every extreme that they name: `acts_in`: real-valued entries. `grad_hidden`: real-valued entries. `acts_hidden`: real-valued entries. `grad_out`: real-valued entries.
All inputs are finite; a program needn't handle non-finite values.
Results may differ from a plain program's by a relative error of at most 0.001.
Values may be sent and summed in bfloat16 or wider, within the bound.
A program may use at most 64 MiB of HBM per device.

v0:
```python
import jax
import jax.numpy as jnp
from jax import lax
from jax.sharding import PartitionSpec as P

D = 8192
FF = 32768


DECAY = 1.0 - 10.0 ** (-0.8)
EPS_SQUARE = 1e-30
CLIP_FLOOR = 0.1


def accumulate(first, second):
    return lax.dot_general(
        first, second, (((0,), (0,)), ((), ())), preferred_element_type=jnp.float32
    )


def finish_update(grad, row_new, col_new):
    return grad / jnp.sqrt(row_new[:, None] * col_new[None, :])


def factored_update(grad, row_state, col_state, rows_total, cols_total):
    square = grad * grad + EPS_SQUARE
    row_part = jnp.sum(square, axis=1)
    col_part = jnp.sum(square, axis=0)
    row_sum = lax.psum(row_part, "col")
    col_sum = lax.psum(col_part, "row")
    row_new = DECAY * row_state + (1.0 - DECAY) * (row_sum / cols_total)
    col_new = DECAY * col_state + (1.0 - DECAY) * (col_sum / rows_total)
    raw = finish_update(grad, row_new, col_new)
    squares = lax.psum(jnp.sum(raw * raw), ("row", "col"))
    rms = jnp.sqrt(squares / (rows_total * cols_total))
    update = (raw / jnp.maximum(CLIP_FLOOR, rms)).astype(jnp.bfloat16)
    return (update, row_new, col_new)


def on_device(
    acts_in,
    grad_hidden,
    acts_hidden,
    grad_out,
    row_state_up,
    col_state_up,
    row_state_down,
    col_state_down,
):
    inputs_whole = lax.all_gather(acts_in, "col", axis=0, tiled=True)
    matching = inputs_whole
    grad_up = accumulate(matching, lax.all_gather(grad_hidden, "row", axis=0, tiled=True))
    outputs_whole = lax.all_gather(grad_out, "row", axis=0, tiled=True)
    matching = outputs_whole
    grad_down = accumulate(lax.all_gather(acts_hidden, "col", axis=0, tiled=True), matching)
    update_up, row_new_up, col_new_up = factored_update(grad_up, row_state_up, col_state_up, D, FF)
    update_down, row_new_down, col_new_down = factored_update(
        grad_down, row_state_down, col_state_down, FF, D
    )
    return (update_up, row_new_up, col_new_up, update_down, row_new_down, col_new_down)


def solution(mesh):
    in_specs = (
        P("col", "row"),
        P("row", "col"),
        P("col", "row"),
        P("row", "col"),
        P("row"),
        P("col"),
        P("row"),
        P("col"),
    )
    out_specs = (P("row", "col"), P("row"), P("col"), P("row", "col"), P("row"), P("col"))
    return jax.shard_map(
        on_device, mesh=mesh, in_specs=in_specs, out_specs=out_specs, check_vma=False
    )
```

profile of v0, /device:TPU:1, one launch (start us, length us, event | category | flops | bytes accessed | tf_op | source)
XLA Modules:
  0.0 549.4 jit_solution(8648597957105147427)
XLA Ops:
  7.2 0.0 all-gather.8.cloned.1.call-start
  7.2 0.7 all-gather.8.cloned.1.call-update
  7.9 0.0 all-gather.6.cloned.1.call-start
  7.9 0.7 all-gather.6.cloned.1.call-update
  8.6 0.0 all-gather.4.cloned.1.call-start
  8.7 0.7 all-gather.4.cloned.1.call-update
  9.4 59.1 %all_gather.12 = bf16[1024,256]{1,0:T(8,128)(2,1)S(1)} all-gather(bf16[64,256]{1,0:T(8,128)(2,1)} %param.8), channel_id=1, replica_groups=mesh['row'=32,'col'=16] {'col'}, dimensions={0}, use_global_device_ids=true | all-gather | bytes 557056 | tf_op jit(solution)/shard_map/all_gather | solution.py:50
  68.4 12.6 %all-gather.8.cloned.1.call-done = bf16[1024,512]{1,0:T(8,128)(2,1)} async-done(((bf16[32,512]{1,0:T(8,128)(2,1)}), bf16[1024,512]{1,0:T(8,128)(2,1)}) %all-gather.8.cloned.1.call-update) | async-done | bytes 1048592 | tf_op jit(solution)/shard_map/all_gather | solution.py:53
  81.0 96.2 %all-gather.6.cloned.1.call-done = bf16[1024,1024]{1,0:T(8,128)(2,1)} async-done(((bf16[64,1024]{1,0:T(8,128)(2,1)}), bf16[1024,1024]{1,0:T(8,128)(2,1)}) %all-gather.6.cloned.1.call-update) | async-done | bytes 2097168 | tf_op jit(solution)/shard_map/all_gather | solution.py:55
  177.2 4.5 fusion.3
  181.6 0.0 copy-start.7
  181.6 0.0 copy-start.6
  181.7 0.0 copy-start.5
  181.7 0.0 copy-start.8
  181.7 61.7 %all-gather.4.cloned.1.call-done = bf16[1024,2048]{1,0:T(8,128)(2,1)} async-done(((bf16[32,2048]{1,0:T(8,128)(2,1)}), bf16[1024,2048]{1,0:T(8,128)(2,1)}) %all-gather.4.cloned.1.call-update) | async-done | bytes 4194320 | tf_op jit(solution)/shard_map/all_gather | solution.py:52
  243.3 3.6 fusion.1
  246.9 130.0 %all-reduce.1 = (f32[2048]{0:T(1024)S(1)}, f32[512]{0:T(512)S(1)}) all-reduce(f32[2048]{0:T(1024)S(1)} %get-tuple-element.9, f32[512]{0:T(512)S(1)} %get-tuple-element.7), channel_id=1, replica_groups=mesh['row'=32,'col'=16] {'row'}, use_global_device_ids=true, to_apply=%region_3.0 | all-reduce | flops 2560 | bytes 20480 | tf_op jit(solution)/shard_map/psum | solution.py:30
  376.9 0.0 copy-done.7
  376.9 0.0 copy-start.3
  376.9 46.8 %all-reduce.2 = (f32[256]{0:T(256)S(1)}, f32[1024]{0:T(1024)S(1)}) all-reduce(f32[256]{0:T(256)S(1)} %get-tuple-element.8, f32[1024]{0:T(1024)S(1)} %get-tuple-element.6), channel_id=1, replica_groups=mesh['row'=32,'col'=16] {'col'}, use_global_device_ids=true, to_apply=%region_1.0 | all-reduce | flops 1280 | bytes 10240 | tf_op jit(solution)/shard_map/psum | solution.py:29
  423.7 0.0 copy-start
  423.7 0.0 copy-done.6
  423.8 0.0 copy-start.2
  423.8 0.0 copy-done.5
  423.8 0.0 copy-start.1
  423.8 0.0 copy-done.8
  423.8 0.0 copy-start.4
  423.8 1.7 multiply_reduce_fusion.1
  425.5 0.0 copy-done
  425.5 1.4 multiply_reduce_fusion
  426.9 110.2 %all-reduce = (f32[]{:T(128)}, f32[]{:T(128)}) all-reduce(f32[]{:T(128)} %multiply_reduce_fusion.1, f32[]{:T(128)} %multiply_reduce_fusion), channel_id=1, replica_groups=mesh['row'=32,'col'=16] {'row','col'}, use_global_device_ids=true, to_apply=%region_5.0 | all-reduce | flops 2 | bytes 16 | tf_op jit(solution)/shard_map/psum | solution.py:34
  537.8 0.0 copy-done.3
  537.8 0.0 copy-done.2
  537.8 2.9 divide_convert_fusion
  541.5 0.0 copy-done.1
  541.5 0.0 copy-done.4
  541.5 1.4 divide_convert_fusion.1
  (4 shorter events, 0.0 us)
Async XLA Ops:
  7.2 73.9 %all-gather.8.cloned.1.call-start = ((), (), s32[]{:S(2)}) async-start(), calls=%async_computation.2 | async-start | bytes 1081344 | tf_op jit(solution)/shard_map/all_gather | solution.py:53
  7.9 169.3 %all-gather.6.cloned.1.call-start = ((), (), s32[]{:S(2)}) async-start(), calls=%async_computation.1 | async-start | bytes 2228224 | tf_op jit(solution)/shard_map/all_gather | solution.py:55
  8.6 234.7 %all-gather.4.cloned.1.call-start = ((), (), s32[]{:S(2)}) async-start(), calls=%async_computation | async-start | bytes 4325376 | tf_op jit(solution)/shard_map/all_gather | solution.py:52
  181.6 195.3 %copy-start.7 = (f32[512]{0:T(512)S(1)}, f32[512]{0:T(512)}, u32[]{:S(2)}) copy-start(f32[512]{0:T(512)} %param.15) | copy-start | bytes 6148
  181.6 242.1 %copy-start.6 = (f32[1024]{0:T(1024)S(1)}, f32[1024]{0:T(1024)}, u32[]{:S(2)}) copy-start(f32[1024]{0:T(1024)} %param.14) | copy-start | bytes 12292
  181.7 242.1 %copy-start.5 = (f32[2048]{0:T(1024)S(1)}, f32[2048]{0:T(1024)}, u32[]{:S(2)}) copy-start(f32[2048]{0:T(1024)} %param.13) | copy-start | bytes 24580
  181.7 242.2 %copy-start.8 = (f32[256]{0:T(256)S(1)}, f32[256]{0:T(256)}, u32[]{:S(2)}) copy-start(f32[256]{0:T(256)} %param.12) | copy-start | bytes 3076
  376.9 160.9 %copy-start.3 = (f32[512]{0:T(512)}, f32[512]{0:T(512)S(1)}, u32[]{:S(2)}) copy-start(f32[512]{0:T(512)S(1)} %multiply_add_fusion.4) | copy-start | bytes 6148
  423.7 1.8 copy-start
  423.8 114.1 %copy-start.2 = (f32[1024]{0:T(1024)}, f32[1024]{0:T(1024)S(1)}, u32[]{:S(2)}) copy-start(f32[1024]{0:T(1024)S(1)} %multiply_add_fusion.3) | copy-start | bytes 12292
  423.8 117.7 %copy-start.1 = (f32[2048]{0:T(1024)}, f32[2048]{0:T(1024)S(1)}, u32[]{:S(2)}) copy-start(f32[2048]{0:T(1024)S(1)} %multiply_add_fusion.2) | copy-start | bytes 24580
  423.8 117.7 %copy-start.4 = (f32[256]{0:T(256)}, f32[256]{0:T(256)S(1)}, u32[]{:S(2)}) copy-start(f32[256]{0:T(256)S(1)} %multiply_add_fusion.5) | copy-start | bytes 3076
Sparse Core Ops, SparseCore 0:
  10.1 70.8 all-gather.7
  84.0 93.0 all-gather.5
  179.3 63.9 all-gather.3
where the time goes:
time: 550 us; the launch traced here: 549 us
  blocking collectives  346 us (63%)
  waiting for transfers between devices  172 us (31%)
  between operations  15.3 us (3%)
  matrix products  8.04 us (1%)
  other arithmetic  7.39 us (1%)
    psum x1, blocking collectives, factored_update(): col_sum = lax.psum(col_part, 'row')  130 us
    psum x1, blocking collectives, factored_update(): squares = lax.psum(jnp.sum(raw * raw), ('row', 'col'))  110 us
    all_gather x1, waiting for transfers between devices, on_device(): lax.all_gather(acts_hidden, 'col', axis=0, tiled=True)  96.2 us
    all_gather x1, waiting for transfers between devices, on_device(): lax.all_gather(grad_hidden, 'row', axis=0, tiled=True)  61.7 us
    all_gather x1, blocking collectives, on_device(): inputs_whole = lax.all_gather(acts_in, 'col', axis=0, tiled=True)  59.1 us
    psum x1, blocking collectives, factored_update(): row_sum = lax.psum(row_part, 'col')  46.8 us
    all_gather x1, waiting for transfers between devices, on_device(): outputs_whole = lax.all_gather(grad_out, 'row', axis=0, tiled=True)  12.6 us
  transfers between devices with their start and end apart: 3, of which 3 were waited for; matrix products, arithmetic and copies ran while one was open for 1% of the time, Pallas kernels for 0%

commit v1 on v0

v1 whole, which is shorter than its diff:
```python
import functools

import jax
import jax.numpy as jnp
from jax import lax
from jax.experimental import pallas as pl
from jax.experimental.pallas import tpu as pltpu
from jax.sharding import PartitionSpec as P

D = 8192
FF = 32768
DECAY = 1.0 - 10.0 ** (-0.8)
EPS_SQUARE = 1e-30
CLIP_FLOOR = 0.1

NB = 16
ROWS = 32
COLS = 16
F32 = jnp.float32
BF16 = jnp.bfloat16
MESH = pl.DeviceIdType.MESH
NSEND = 112


def mod(a, n):
    return lax.rem(a + n, n)


def kernel(
    ai_in, h_in, ah_in, o_in, rsu_in, csu_in, rsd_in, csd_in,
    uu_out, rnu_out, cnu_out, ud_out, rnd_out, cnd_out,
    ai, ah, h, o, gu, gd, uu, ud, rbu, rbd,
    rstate, cstate, rnew, cnew, rpart, cpart, rbuf, cbuf, tpart, tbuf1, tpart2, tbuf2,
    ai_sem, ah_sem, h_sem, o_sem, hs_sem, os_sem, send_sem, loc_sem, out_sem,
    r_recv, c_recv, r_send, c_send, t1_recv, t1_send, t2_recv, t2_send,
):
    r = lax.axis_index("row")
    c = lax.axis_index("col")
    core = lax.rem(r, 2)
    x = lax.rem(r // 2, 4)
    p = r // 8
    y = lax.rem(c, 4)
    zh = c // 4
    s = 1 - 2 * core

    def row_at(zl_, x_, core_):
        return (zl_ * 8 + x_ * 2 + core_, c)

    def col_at(zh_, y_):
        return (r, zh_ * 4 + y_)

    xf, xb = mod(x + s, 4), mod(x - s, 4)
    yf, yb = mod(y + s, 4), mod(y - s, 4)
    zf, zb = mod(zh + s, 4), mod(zh - s, 4)
    x_f, x_b = row_at(p, xf, core), row_at(p, xb, core)
    y_f, y_b = col_at(zh, yf), col_at(zh, yb)
    z_f, z_b = col_at(zf, y), col_at(zb, y)
    l_f, l_b = row_at(mod(p + 1, 4), x, core), row_at(mod(p - 1, 4), x, core)
    sib = row_at(p, x, 1 - core)

    barrier = pltpu.get_barrier_semaphore()
    for dev in (x_f, x_b, y_f, y_b, z_f, z_b, l_f, l_b, sib):
        pl.semaphore_signal(barrier, inc=1, device_id=dev, device_id_type=MESH)
    pl.semaphore_wait(barrier, 9)

    sends = []
    nsend = [0]

    def send(src, dst, recv, like, dev, conds=()):
        k = nsend[0]
        nsend[0] += 1
        pltpu.make_async_remote_copy(src, dst, send_sem.at[k], recv, dev, MESH).start()
        sends.append((like, k, conds))

    def when(conds, f):
        if not conds:
            f()
        else:
            pl.when(conds[0])(lambda: when(conds[1:], f))

    def arrived(dst, recv, like=None):
        pltpu.make_async_remote_copy(dst, dst, send_sem.at[0], recv, sib, MESH).wait_recv()

    def hslot(b):
        return h.at[b, core], h_sem.at[b], lambda: h.at[0, 0]

    def oslot(b):
        return o.at[b, core], o_sem.at[b], lambda: o.at[0, 0]

    def aislot(b):
        return ai.at[b], ai_sem.at[b], lambda: ai.at[0]

    def ahslot(b):
        return ah.at[b], ah_sem.at[b], lambda: ah.at[0]

    not_last, not_first = p < 3, p > 0

    own_r, own_c = p * 4 + x, c
    ROWG = ((h_in, hslot), (o_in, oslot))

    def line_own():
        @pl.when(not_last)
        def _():
            for src, slot in ROWG:
                send(src, *slot(own_r), l_f, (not_last,))

        @pl.when(not_first)
        def _():
            for src, slot in ROWG:
                send(src, *slot(own_r), l_b, (not_first,))

    line_own()
    for dev in (z_f, z_b):
        send(ai_in, *aislot(own_c), dev)
    for src, slot in ROWG:
        for dev in (x_f, x_b):
            send(src, *slot(own_r), dev)
    for src, slot in ((ai_in, aislot), (ah_in, ahslot)):
        for dev in (y_f, y_b):
            send(src, *slot(own_c), dev)
    for dev in (z_f, z_b):
        send(ah_in, *ahslot(own_c), dev)

    local = [
        pltpu.make_async_copy(ai_in, ai.at[own_c], loc_sem.at[0]),
        pltpu.make_async_copy(ah_in, ah.at[own_c], loc_sem.at[1]),
        pltpu.make_async_copy(h_in, h.at[own_r, core], loc_sem.at[2]),
        pltpu.make_async_copy(o_in, o.at[own_r, core], loc_sem.at[3]),
        pltpu.make_async_copy(rsu_in, rstate.at[pl.ds(8, 2)], loc_sem.at[4]),
        pltpu.make_async_copy(rsd_in, rstate.at[pl.ds(0, 8)], loc_sem.at[5]),
        pltpu.make_async_copy(csu_in, cstate.at[pl.ds(0, 16)], loc_sem.at[6]),
        pltpu.make_async_copy(csd_in, cstate.at[pl.ds(16, 4)], loc_sem.at[7]),
    ]
    for copy in local:
        copy.start()

    def line(d):
        left, right = p >= d, p + d <= 3

        @pl.when(left)
        def _():
            b = (p - d) * 4 + x
            for _, slot in ROWG:
                arrived(*slot(b))
            if d < 3:
                @pl.when(not_last)
                def _():
                    for _, slot in ROWG:
                        send(slot(b)[0], *slot(b), l_f, (left, not_last))
            for _, slot in ROWG:
                for dev in (x_f, x_b):
                    send(slot(b)[0], *slot(b), dev, (left,))

        @pl.when(right)
        def _():
            b = (p + d) * 4 + x
            for _, slot in ROWG:
                arrived(*slot(b))
            if d < 3:
                @pl.when(not_first)
                def _():
                    for _, slot in ROWG:
                        send(slot(b)[0], *slot(b), l_b, (right, not_first))
            for _, slot in ROWG:
                for dev in (x_f, x_b):
                    send(slot(b)[0], *slot(b), dev, (right,))

    def x_forward(d):
        def one(q, conds):
            b = q * 4 + xb
            for _, slot in ROWG:
                arrived(*slot(b))
            for _, slot in ROWG:
                send(slot(b)[0], *slot(b), x_f, conds)

        if d == 0:
            one(p, ())
        else:
            left, right = p >= d, p + d <= 3
            pl.when(left)(lambda: one(p - d, (left,)))
            pl.when(right)(lambda: one(p + d, (right,)))

    def to_sibling(d):
        def one(q, conds):
            for b in (q * 4 + xf, q * 4 + mod(x + 2, 4)):
                for _, slot in ROWG:
                    arrived(*slot(b))
            part = h.at[pl.ds(q * 4, 4), core]
            send(part, part, hs_sem.at[q], lambda: h.at[pl.ds(0, 4), 0], sib, conds)
            part = o.at[pl.ds(q * 4, 4), core]
            send(part, part, os_sem.at[q], lambda: o.at[pl.ds(0, 4), 0], sib, conds)

        if d == 0:
            local[2].wait()
            local[3].wait()
            one(p, ())
        else:
            left, right = p >= d, p + d <= 3
            pl.when(left)(lambda: one(p - d, (left,)))
            pl.when(right)(lambda: one(p + d, (right,)))

    def zy(slot, b):
        arrived(*slot(b))
        for dev in (y_f, y_b):
            send(slot(b)[0], *slot(b), dev)

    def z_first(slot):
        b = zb * 4 + y
        arrived(*slot(b))
        send(slot(b)[0], *slot(b), z_f)
        for dev in (y_f, y_b):
            send(slot(b)[0], *slot(b), dev)
        zy(slot, zf * 4 + y)

    def z_second(slot):
        zy(slot, mod(zh + 2, 4) * 4 + y)

    def y_forward(slot, q):
        b = q * 4 + yb
        arrived(*slot(b))
        send(slot(b)[0], *slot(b), y_f)

    def y_last(slot, q):
        for b in (q * 4 + yf, q * 4 + mod(y + 2, 4)):
            arrived(*slot(b))

    z2 = mod(zh + 2, 4)
    line(1)
    z_first(aislot)
    x_forward(0)
    y_forward(aislot, zh)
    y_forward(ahslot, zh)
    line(2)
    x_forward(1)
    z_second(aislot)
    y_forward(aislot, zb)
    y_forward(aislot, zf)
    to_sibling(0)
    line(3)
    x_forward(2)
    z_first(ahslot)
    y_forward(aislot, z2)
    x_forward(3)
    to_sibling(1)
    y_forward(ahslot, zb)
    y_forward(ahslot, zf)
    to_sibling(2)
    to_sibling(3)

    local[0].wait()
    for q in (zh, zb, zf, z2):
        y_last(aislot, q)
    for q in range(4):
        part = h.at[pl.ds(q * 4, 4), 1 - core]
        arrived(part, hs_sem.at[q])
        part = o.at[pl.ds(q * 4, 4), 1 - core]
        arrived(part, os_sem.at[q])

    def product(a, b):
        return lax.dot_general(a, b, (((0,), (0,)), ((), ())), preferred_element_type=F32)

    lhs = ai[...].reshape(1024, 256)

    def up_tile(n, carry):
        cols = pl.ds(pl.multiple_of(n * 512, 512), 512)
        gu[:, cols] = product(lhs, h[:, :, :, cols].reshape(1024, 512))
        return carry

    z_second(ahslot)
    lax.fori_loop(0, 4, up_tile, 0)
    y_forward(ahslot, z2)

    def up_squares(j, sums):
        cols = pl.ds(pl.multiple_of(j * 128, 128), 128)
        g = gu[:, cols]
        sq = g * g + EPS_SQUARE
        cpart[pl.ds(j, 1), :] = jnp.sum(sq, axis=0, keepdims=True)
        return sums + sq

    sums = lax.fori_loop(0, 16, up_squares, jnp.zeros((256, 128), F32))
    for a in range(2):
        rpart[8 + a : 9 + a, :] = jnp.sum(
            jnp.transpose(sums[a * 128 : a * 128 + 128]), axis=0, keepdims=True
        )

    local[1].wait()

    def down_part(q, first):
        b = pl.ds(q * 4, 4)
        term = product(ah[b].reshape(256, 1024), o[b].reshape(256, 512))
        if first:
            gd[...] = term
        else:
            gd[...] += term

    for i, q in enumerate((zh, zb, zf, z2)):
        y_last(ahslot, q)
        down_part(q, i == 0)

    ctotal = jnp.zeros((8, 512), F32)
    for a in range(8):
        g = gd[a * 128 : a * 128 + 128, :]
        sq = g * g + EPS_SQUARE
        ctotal = ctotal + jnp.sum(sq.reshape(16, 8, 512), axis=0)
        lanes = sq[:, 0:128] + sq[:, 128:256] + sq[:, 256:384] + sq[:, 384:512]
        rpart[a : a + 1, :] = jnp.sum(jnp.transpose(lanes), axis=0, keepdims=True)
    csum = jnp.sum(ctotal, axis=0, keepdims=True)
    for j in range(4):
        cpart[16 + j : 17 + j, :] = csum[:, j * 128 : j * 128 + 128]

    def exchange(part, buf, ssem, rsem, n, me, where):
        def start(k, carry):
            to = mod(me + k, n)
            pltpu.make_async_remote_copy(
                part, buf.at[me], ssem.at[k], rsem.at[me], where(to), MESH
            ).start()
            return carry

        lax.fori_loop(1, n, start, 0)

    def finish(part, buf, ssem, rsem, n, me):
        def wait(k, carry):
            frm = mod(me + k, n)
            pltpu.make_async_remote_copy(
                buf.at[frm], buf.at[frm], ssem.at[k], rsem.at[frm], sib, MESH
            ).wait_recv()
            return carry

        lax.fori_loop(1, n, wait, 0)

    def finish_sends(part, buf, ssem, rsem, n, me):
        def wait(k, carry):
            pltpu.make_async_remote_copy(
                part, buf.at[me], ssem.at[k], rsem.at[me], sib, MESH
            ).wait_send()
            return carry

        lax.fori_loop(1, n, wait, 0)

    to_row = lambda k: (k, c)
    to_col = lambda k: (r, k)
    exchange(cpart, cbuf, c_send, c_recv, ROWS, r, to_row)
    exchange(rpart, rbuf, r_send, r_recv, COLS, c, to_col)
    cbuf[r] = cpart[...]
    rbuf[c] = rpart[...]

    for like, k, conds in sends:
        when(conds, lambda: pltpu.make_async_remote_copy(
            like(), like(), send_sem.at[k], loc_sem.at[0], sib, MESH).wait_send())
    for copy in local[4:]:
        copy.wait()

    finish(rpart, rbuf, r_send, r_recv, COLS, c)
    row_sum = jnp.sum(rbuf[...], axis=0)
    keep, take = DECAY, 1.0 - DECAY
    rn_d = keep * rstate[0:8, :] + take * (row_sum[0:8] / D)
    rn_u = keep * rstate[8:10, :] + take * (row_sum[8:10] / FF)
    rnew[0:8, :] = rn_d
    rnew[8:10, :] = rn_u
    rroot_d = lax.rsqrt(rn_d)
    rroot_u = lax.rsqrt(rn_u)
    for a in range(8):
        rbd[a * 128 : a * 128 + 128, :] = jnp.transpose(
            jnp.broadcast_to(rroot_d[a : a + 1, :], (128, 128))
        )
    for a in range(2):
        rbu[a * 128 : a * 128 + 128, :] = jnp.transpose(
            jnp.broadcast_to(rroot_u[a : a + 1, :], (128, 128))
        )

    finish(cpart, cbuf, c_send, c_recv, ROWS, r)
    col_sum = jnp.sum(cbuf[...], axis=0)
    cn_u = keep * cstate[0:16, :] + take * (col_sum[0:16] / D)
    cn_d = keep * cstate[16:20, :] + take * (col_sum[16:20] / FF)
    cnew[0:16, :] = cn_u
    cnew[16:20, :] = cn_d
    cstate[0:16, :] = lax.rsqrt(cn_u)
    cstate[16:20, :] = lax.rsqrt(cn_d)

    outs = [
        pltpu.make_async_copy(rnew.at[pl.ds(8, 2)], rnu_out, out_sem.at[0]),
        pltpu.make_async_copy(rnew.at[pl.ds(0, 8)], rnd_out, out_sem.at[1]),
        pltpu.make_async_copy(cnew.at[pl.ds(0, 16)], cnu_out, out_sem.at[2]),
        pltpu.make_async_copy(cnew.at[pl.ds(16, 4)], cnd_out, out_sem.at[3]),
        pltpu.make_async_copy(uu, uu_out, out_sem.at[4]),
        pltpu.make_async_copy(ud, ud_out, out_sem.at[5]),
    ]
    for copy in outs[:4]:
        copy.start()

    def up_raw(j, total):
        cols = pl.ds(pl.multiple_of(j * 128, 128), 128)
        raw = gu[:, cols] * rbu[...] * cstate[pl.ds(j, 1), :]
        return total + jnp.sum((raw * raw).reshape(32, 8, 128), axis=0)

    tu = lax.fori_loop(0, 16, up_raw, jnp.zeros((8, 128), F32))

    def down_raw(a, total):
        rows = pl.ds(pl.multiple_of(a * 128, 128), 128)
        for j in range(4):
            cols = slice(j * 128, j * 128 + 128)
            raw = gd[rows, cols] * rbd[rows, :] * cstate[16 + j : 17 + j, :]
            total = total + jnp.sum((raw * raw).reshape(16, 8, 128), axis=0)
        return total

    td = lax.fori_loop(0, 8, down_raw, jnp.zeros((8, 128), F32))
    tpart[0] = tu
    tpart[1] = td

    exchange(tpart, tbuf1, t1_send, t1_recv, COLS, c, to_col)
    tbuf1[c] = tpart[...]
    finish_sends(rpart, rbuf, r_send, r_recv, COLS, c)
    finish_sends(cpart, cbuf, c_send, c_recv, ROWS, r)
    finish(tpart, tbuf1, t1_send, t1_recv, COLS, c)
    tpart2[...] = jnp.sum(tbuf1[...], axis=0)
    exchange(tpart2, tbuf2, t2_send, t2_recv, ROWS, r, to_row)
    tbuf2[r] = tpart2[...]
    finish_sends(tpart, tbuf1, t1_send, t1_recv, COLS, c)
    finish(tpart2, tbuf2, t2_send, t2_recv, ROWS, r)
    totals = jnp.sum(tbuf2[...], axis=0)
    size = float(D) * float(FF)

    def scale_of(t):
        total = jnp.sum(jnp.sum(t, axis=0, keepdims=True), axis=1, keepdims=True)
        return 1.0 / jnp.maximum(CLIP_FLOOR, jnp.sqrt(total / size))

    scale_u = scale_of(totals[0])
    scale_d = scale_of(totals[1])
    cstate[0:16, :] = cstate[0:16, :] * scale_u
    cstate[16:20, :] = cstate[16:20, :] * scale_d

    def up_write(j, carry):
        cols = pl.ds(pl.multiple_of(j * 128, 128), 128)
        uu[:, cols] = (gu[:, cols] * rbu[...] * cstate[pl.ds(j, 1), :]).astype(BF16)
        return carry

    lax.fori_loop(0, 16, up_write, 0)
    outs[4].start()

    def down_write(a, carry):
        rows = pl.ds(pl.multiple_of(a * 128, 128), 128)
        for j in range(4):
            cols = slice(j * 128, j * 128 + 128)
            ud[rows, cols] = (
                gd[rows, cols] * rbd[rows, :] * cstate[16 + j : 17 + j, :]
            ).astype(BF16)
        return carry

    lax.fori_loop(0, 8, down_write, 0)
    outs[5].start()
    finish_sends(tpart2, tbuf2, t2_send, t2_recv, ROWS, r)
    for copy in outs:
        copy.wait()


def on_device(ai, h, ah, o, rsu, csu, rsd, csd):
    dma = pltpu.SemaphoreType.DMA
    any_ = pl.BlockSpec(memory_space=pl.ANY)

    res = pl.pallas_call(
        kernel,
        out_shape=(
            jax.ShapeDtypeStruct((256, 2048), BF16),
            jax.ShapeDtypeStruct((2, 128), F32),
            jax.ShapeDtypeStruct((16, 128), F32),
            jax.ShapeDtypeStruct((1024, 512), BF16),
            jax.ShapeDtypeStruct((8, 128), F32),
            jax.ShapeDtypeStruct((4, 128), F32),
        ),
        in_specs=[any_] * 8,
        out_specs=[any_] * 6,
        scratch_shapes=[
            pltpu.VMEM((NB, 64, 256), BF16),
            pltpu.VMEM((NB, 64, 1024), BF16),
            pltpu.VMEM((NB, 2, 32, 2048), BF16),
            pltpu.VMEM((NB, 2, 32, 512), BF16),
            pltpu.VMEM((256, 2048), F32),
            pltpu.VMEM((1024, 512), F32),
            pltpu.VMEM((256, 2048), BF16),
            pltpu.VMEM((1024, 512), BF16),
            pltpu.VMEM((256, 128), F32),
            pltpu.VMEM((1024, 128), F32),
            pltpu.VMEM((16, 128), F32),
            pltpu.VMEM((24, 128), F32),
            pltpu.VMEM((16, 128), F32),
            pltpu.VMEM((24, 128), F32),
            pltpu.VMEM((16, 128), F32),
            pltpu.VMEM((24, 128), F32),
            pltpu.VMEM((COLS, 16, 128), F32),
            pltpu.VMEM((ROWS, 24, 128), F32),
            pltpu.VMEM((2, 8, 128), F32),
            pltpu.VMEM((COLS, 2, 8, 128), F32),
            pltpu.VMEM((2, 8, 128), F32),
            pltpu.VMEM((ROWS, 2, 8, 128), F32),
            dma((NB,)), dma((NB,)), dma((NB,)), dma((NB,)), dma((4,)), dma((4,)),
            dma((NSEND,)), dma((8,)), dma((6,)),
            dma((COLS,)), dma((ROWS,)), dma((COLS,)), dma((ROWS,)),
            dma((COLS,)), dma((COLS,)), dma((ROWS,)), dma((ROWS,)),
        ],
        compiler_params=pltpu.CompilerParams(
            collective_id=0, has_side_effects=True, vmem_limit_bytes=40 * 1024 * 1024
        ),
        cost_estimate=pl.CostEstimate(
            flops=2 * 2 * 1024 * 256 * 2048, bytes_accessed=3 << 20, transcendentals=0
        ),
    )(ai, h, ah, o, rsu.reshape(2, 128), csu.reshape(16, 128), rsd.reshape(8, 128), csd.reshape(4, 128))
    uu, rnu, cnu, ud, rnd, cnd = res
    return (uu, rnu.reshape(256), cnu.reshape(2048), ud, rnd.reshape(1024), cnd.reshape(512))


def solution(mesh):
    in_specs = (
        P("col", "row"),
        P("row", "col"),
        P("col", "row"),
        P("row", "col"),
        P("row"),
        P("col"),
        P("row"),
        P("col"),
    )
    out_specs = (P("row", "col"), P("row"), P("col"), P("row", "col"), P("row"), P("col"))
    return jax.shard_map(
        on_device, mesh=mesh, in_specs=in_specs, out_specs=out_specs, check_vma=False
    )
```

time: 550 us -> 112 us (0.20)
  blocking collectives: 346 us -> 0 us
  waiting for transfers between devices: 172 us -> 0 us
  Pallas kernels: 0 us -> 102 us
  between operations: 15.3 us -> 0.68 us
  local copies, waits for them, and re-layouts: 0.04 us -> 8.98 us
  matrix products: 8.04 us -> 0 us
  other arithmetic: 7.39 us -> 0 us
    psum x3 -> x0, blocking collectives: 287 us -> none  [the longest x1 130 us: factored_update(): col_sum = lax.psum(col_part, 'row')]
    all_gather x3 -> x0, waiting for transfers between devices: 170 us -> none  [the longest x1 96.2 us: on_device(): lax.all_gather(acts_hidden, 'col', axis=0, tiled=True)]
    pallas_call x0 -> x1, Pallas kernels: none -> 102 us  [on_device(): pl.pallas_call(kernel, out_shape=(jax.ShapeDtypeStruct((256, 2048), BF16)...]
    all_gather x1 -> x0, blocking collectives: 59.1 us -> none  [on_device(): inputs_whole = lax.all_gather(acts_in, 'col', axis=0, tiled=True)]
    unnamed x18 -> x22, local copies, waits for them, and re-layouts: 0.04 us -> 8.98 us
    dot_general x2 -> x0, matrix products: 8.04 us -> none  [accumulate(): lax.dot_general(first, second, (((0,), (0,)), ((), ())), preferred_elemen...]
  transfers between devices with their start and end apart: 3 -> 0, of which waited for: 3 -> 0; matrix products, arithmetic and copies ran while one was open for 1% -> 0% of each run, Pallas kernels for 0% -> 0%
where the time goes in v1:
time: 112 us
  Pallas kernels  102 us (91%)
  local copies, waits for them, and re-layouts  8.98 us (8%)
    pallas_call x1, Pallas kernels, on_device(): pl.pallas_call(kernel, out_shape=(jax.ShapeDtypeStruct((256, 2048), BF16)...  102 us
    unnamed x22, local copies, waits for them, and re-layouts  8.98 us

profile of v1, /device:TPU:1, one launch (start us, length us, event | category | flops | bytes accessed | tf_op | source)
XLA Modules:
  0.0 111.9 jit_solution(16543382859814011207)
XLA Ops:
  0.6 0.0 copy-start.5
  0.6 0.0 copy-start.6
  0.7 0.0 copy-start.7
  0.7 0.7 copy-done.5
  1.3 0.0 copy-done.6
  1.3 0.0 copy-done.7
  1.3 0.0 copy-start
  1.3 0.9 copy-done
  2.3 0.0 copy-start.1
  2.3 0.9 copy-done.1
  3.2 0.0 copy-start.2
  3.2 0.8 copy-done.2
  3.9 0.0 copy-start.3
  3.9 0.8 copy-done.3
  4.7 0.0 copy-start.4
  4.7 0.7 copy-done.4
  5.4 102.3 %shard_map.127 = (bf16[256,2048]{1,0:T(8,128)(2,1)S(1)}, f32[2,128]{1,0:T(2,128)S(1)}, f32[16,128]{1,0:T(8,128)S(1)}, bf16[1024,512]{1,0:T(8,128)(2,1)S(1)}, f32[8,128]{1,0:T(8,128)S(1)}, /*index=5*/f32[4,128]{1,0:T(4,128)S(1)}) custom-call(bf16[64,256]{1,0:T(8,128)(2,1)S(1)} %copy-done.2, bf16[32,2048]{1,0:T(8,128)(2,1)S(1)} %copy-done, ...), custom_call_target="tpu_custom_call" | custom-call | flops 2147483648 | bytes 3145728 | tf_op jit(solution)/shard_map/pallas_call | solution.py:460
  107.6 1.0 copy.20
  108.6 0.6 copy.21
  109.2 0.6 copy.22
  109.8 1.0 copy.23
  110.7 0.6 copy.24
  111.3 0.6 copy.25
Async XLA Ops:
  0.6 0.7 copy-start.5
  0.6 0.7 copy-start.6
  0.7 0.7 copy-start.7
  1.3 0.9 copy-start
  2.3 0.9 copy-start.1
  3.2 0.8 copy-start.2
  3.9 0.8 copy-start.3
  4.7 0.7 copy-start.4

commit v2 on v0

v2 whole, which is shorter than its diff:
```python
import jax
import jax.numpy as jnp
from jax import lax
from jax.experimental import pallas as pl
from jax.experimental.pallas import tpu as pltpu
from jax.sharding import PartitionSpec as P

D = 8192
FF = 32768
DECAY = 1.0 - 10.0 ** (-0.8)
EPS_SQUARE = 1e-30
CLIP_FLOOR = 0.1

NB = 16
ROWS = 32
COLS = 16
AHC = 2
F32 = jnp.float32
BF16 = jnp.bfloat16
MESH = pl.DeviceIdType.MESH
NSEND = 200
VMEM_MB = 57


def mod(a, n):
    return lax.rem(a + n, n)


def kernel(
    ai_in, h_in, ah_in, o_in, rsu_in, csu_in, rsd_in, csd_in,
    uu, rnu, cnu, ud, rnd, cnd,
    ai, ah, h, o, gu, gd, rbu, rbd, rsu, csu, rsd, csd, cru, crd,
    rpu, cpu, cpu2, rpd, cpd, rbufu, cbufu, cbufu2, rbufd, cbufd, tp1, tbuf1, tp2, tbuf2,
    ai_sem, ah_sem, h_sem, o_sem, hs_sem, os_sem, send_sem, loc_sem,
    rd_sem, cd_sem, ru_sem, cu1_sem, cu2_sem, t1_sem, t2_sem,
):
    r = lax.axis_index("row")
    c = lax.axis_index("col")
    core = lax.rem(r, 2)
    x = lax.rem(r // 2, 4)
    p = r // 8
    y = lax.rem(c, 4)
    zh = c // 4
    s = 1 - 2 * core

    def row_at(zl_, x_, core_):
        return (zl_ * 8 + x_ * 2 + core_, c)

    def col_at(zh_, y_):
        return (r, zh_ * 4 + y_)

    zf, zb, z2 = mod(zh + s, 4), mod(zh - s, 4), mod(zh + 2, 4)
    xs = [row_at(p, mod(x + i, 4), core) for i in (2, 1, 3)]
    ys = [col_at(zh, mod(y + i, 4)) for i in (2, 1, 3)]
    z_f, z_b = col_at(zf, y), col_at(zb, y)
    l_f, l_b = row_at(mod(p + 1, 4), x, core), row_at(mod(p - 1, 4), x, core)
    sib = row_at(p, x, 1 - core)

    barrier = pltpu.get_barrier_semaphore()
    for dev in (z_f, z_b, l_f, l_b, *xs, *ys, sib):
        pl.semaphore_signal(barrier, inc=1, device_id=dev, device_id_type=MESH)
    pl.semaphore_wait(barrier, 11)

    sends = []

    def send(src, dst, recv, like, dev, conds=()):
        k = len(sends)
        pltpu.make_async_remote_copy(src, dst, send_sem.at[k], recv, dev, MESH).start()
        sends.append((like, conds))

    def when(conds, f):
        if not conds:
            f()
        else:
            pl.when(conds[0])(lambda: when(conds[1:], f))

    def arrived(dst, recv, like=None):
        pltpu.make_async_remote_copy(dst, dst, send_sem.at[0], recv, sib, MESH).wait_recv()

    def hslot(b):
        return h.at[b, core], h_sem.at[b], lambda: h.at[0, 0]

    def oslot(b):
        return o.at[b, core], o_sem.at[b], lambda: o.at[0, 0]

    def aislot(b):
        return ai.at[b], ai_sem.at[b], lambda: ai.at[0]

    AHT = 64 // AHC

    def ahslot(t):
        part = pl.ds(t * AHT, AHT)

        def slot(b):
            return ah.at[b, part], ah_sem.at[b, t], lambda: ah.at[0, part]

        return slot

    not_last, not_first = p < 3, p > 0
    own_r, own_c = p * 4 + x, c
    ah_own = [ah_in.at[pl.ds(t * AHT, AHT)] for t in range(AHC)]

    def line_own(src, slot):
        @pl.when(not_last)
        def _():
            send(src, *slot(own_r), l_f, (not_last,))

        @pl.when(not_first)
        def _():
            send(src, *slot(own_r), l_b, (not_first,))

    def spread(src, slot, b, devs, conds=()):
        for dev in devs:
            send(src, *slot(b), dev, conds)

    line_own(h_in, hslot)
    spread(ah_own[0], ahslot(0), own_c, (z_f, z_b))
    line_own(o_in, oslot)
    spread(h_in, hslot, own_r, xs)
    for t in range(AHC):
        spread(ah_own[t], ahslot(t), own_c, ys)
    spread(o_in, oslot, own_r, xs)
    spread(ai_in, aislot, own_c, ys)

    local = [
        pltpu.make_async_copy(ai_in, ai.at[own_c], loc_sem.at[0]),
        pltpu.make_async_copy(ah_in, ah.at[own_c], loc_sem.at[1]),
        pltpu.make_async_copy(h_in, h.at[own_r, core], loc_sem.at[2]),
        pltpu.make_async_copy(o_in, o.at[own_r, core], loc_sem.at[3]),
        pltpu.make_async_copy(rsu_in, rsu, loc_sem.at[4]),
        pltpu.make_async_copy(rsd_in, rsd, loc_sem.at[5]),
        pltpu.make_async_copy(csu_in, csu, loc_sem.at[6]),
        pltpu.make_async_copy(csd_in, csd, loc_sem.at[7]),
    ]
    for copy in local:
        copy.start()

    def line(slot, d):
        left, right = p >= d, p + d <= 3

        def one(b, further, dev, conds):
            arrived(*slot(b))
            if d < 3:
                @pl.when(further)
                def _():
                    send(slot(b)[0], *slot(b), dev, conds + (further,))
            spread(slot(b)[0], slot, b, xs, conds)

        pl.when(left)(lambda: one((p - d) * 4 + x, not_last, l_f, (left,)))
        pl.when(right)(lambda: one((p + d) * 4 + x, not_first, l_b, (right,)))

    def z_one(slot, zz, onward=False):
        b = zz * 4 + y
        arrived(*slot(b))
        if onward:
            send(slot(b)[0], *slot(b), z_f)
        spread(slot(b)[0], slot, b, ys)

    def z_first(slot):
        z_one(slot, zb, True)
        z_one(slot, zf)

    def z_second(slot):
        z_one(slot, z2)

    def to_sibling(d):
        def one(q, conds):
            for i in (1, 3, 2):
                b = q * 4 + mod(x + i, 4)
                arrived(*hslot(b))
                arrived(*oslot(b))
            for buf, sem in ((h, hs_sem), (o, os_sem)):
                part = buf.at[pl.ds(q * 4, 4), core]
                send(part, part, sem.at[q], lambda buf=buf: buf.at[pl.ds(0, 4), 0], sib, conds)

        if d == 0:
            local[2].wait()
            local[3].wait()
            one(p, ())
        else:
            left, right = p >= d, p + d <= 3
            pl.when(left)(lambda: one(p - d, (left,)))
            pl.when(right)(lambda: one(p + d, (right,)))

    def y_last(slot, q):
        for i in (1, 3, 2):
            arrived(*slot(q * 4 + mod(y + i, 4)))

    line(hslot, 1)
    z_first(ahslot(0))
    spread(ah_own[1], ahslot(1), own_c, (z_f, z_b))
    line(oslot, 1)
    line(hslot, 2)
    z_first(ahslot(1))
    spread(ai_in, aislot, own_c, (z_f, z_b))
    line(oslot, 2)
    z_second(ahslot(0))
    line(hslot, 3)
    to_sibling(0)
    line(oslot, 3)
    z_first(aislot)
    z_second(ahslot(1))
    to_sibling(1)
    z_second(aislot)
    to_sibling(2)
    to_sibling(3)
    def product(a, b):
        return lax.dot_general(a, b, (((0,), (0,)), ((), ())), preferred_element_type=F32)

    def start(part, buf, sem, n, me, where):
        def one(k, carry):
            pltpu.make_async_remote_copy(
                part, buf.at[me], sem.at[1, k], sem.at[0, me], where(mod(me + k, n)), MESH
            ).start()
            return carry

        lax.fori_loop(1, n, one, 0)
        buf[me] = part[...]

    def finish(buf, sem, n, me):
        def one(k, carry):
            frm = mod(me + k, n)
            pltpu.make_async_remote_copy(
                buf.at[frm], buf.at[frm], sem.at[1, k], sem.at[0, frm], sib, MESH
            ).wait_recv()
            return carry

        lax.fori_loop(1, n, one, 0)
        return jnp.sum(buf[...], axis=0)

    def finish_sends(part, sem, n):
        def one(k, carry):
            pltpu.make_async_remote_copy(
                part, part, sem.at[1, k], sem.at[0, 0], sib, MESH
            ).wait_send()
            return carry

        lax.fori_loop(1, n, one, 0)

    to_row = lambda k: (k, c)
    to_col = lambda k: (r, k)
    in_x = lambda k: (p * 8 + k, c)
    in_line = lambda k: (k * 8 + lax.rem(r, 8), c)
    in_plane = lambda k: (p * 8 + lax.rem(k, 8), zh * 4 + k // 8)
    in_z = lambda k: (lax.rem(k, 4) * 8 + lax.rem(r, 8), (k // 4) * 4 + y)


    local[1].wait()
    for q in range(4):
        arrived(o.at[pl.ds(q * 4, 4), 1 - core], os_sem.at[q])
    for q in (zh, zb, zf, z2):
        for t in range(AHC):
            y_last(ahslot(t), q)
    lhs_down = ah[...].reshape(1024, 1024)
    gd[...] = product(lhs_down, o[...].reshape(1024, 512))

    ctotal = jnp.zeros((8, 512), F32)
    for a in range(8):
        g = gd[a * 128 : a * 128 + 128, :]
        sq = g * g + EPS_SQUARE
        ctotal = ctotal + jnp.sum(sq.reshape(16, 8, 512), axis=0)
        lanes = sq[:, 0:128] + sq[:, 128:256] + sq[:, 256:384] + sq[:, 384:512]
        rpd[a : a + 1, :] = jnp.sum(jnp.transpose(lanes), axis=0, keepdims=True)
    csum = jnp.sum(ctotal, axis=0, keepdims=True)
    for j in range(4):
        cpd[j : j + 1, :] = csum[:, j * 128 : j * 128 + 128]

    start(rpd, rbufd, rd_sem, COLS, c, to_col)
    start(cpd, cbufd, cd_sem, ROWS, r, to_row)

    local[0].wait()
    for q in range(4):
        arrived(h.at[pl.ds(q * 4, 4), 1 - core], hs_sem.at[q])
    for q in (zh, zb, zf, z2):
        y_last(aislot, q)
    lhs = ai[...].reshape(1024, 256)

    def up_tile(n, carry):
        cols = pl.ds(pl.multiple_of(n * 512, 512), 512)
        gu[:, cols] = product(lhs, h[:, :, :, cols].reshape(1024, 512))
        return carry

    lax.fori_loop(0, 4, up_tile, 0)

    def up_squares(j, sums):
        cols = pl.ds(pl.multiple_of(j * 128, 128), 128)
        g = gu[:, cols]
        sq = g * g + EPS_SQUARE
        cpu[pl.ds(j, 1), :] = jnp.sum(sq, axis=0, keepdims=True)
        return sums + sq

    sums = lax.fori_loop(0, 16, up_squares, jnp.zeros((256, 128), F32))
    for a in range(2):
        rpu[a : a + 1, :] = jnp.sum(
            jnp.transpose(sums[a * 128 : a * 128 + 128]), axis=0, keepdims=True
        )


    start(cpu, cbufu, cu1_sem, 8, x * 2 + core, in_x)
    start(rpu, rbufu, ru_sem, COLS, c, to_col)

    cpu2[...] = finish(cbufu, cu1_sem, 8, x * 2 + core)
    start(cpu2, cbufu2, cu2_sem, 4, p, in_line)

    for k, (like, conds) in enumerate(sends):
        when(conds, lambda: pltpu.make_async_remote_copy(
            like(), like(), send_sem.at[k], loc_sem.at[0], sib, MESH).wait_send())
    for copy in local[4:]:
        copy.wait()

    keep, take = DECAY, 1.0 - DECAY
    cn = keep * csd[...] + take * (finish(cbufd, cd_sem, ROWS, r) / FF)
    cnd[...] = cn
    crd[...] = lax.rsqrt(cn)
    rn = keep * rsd[...] + take * (finish(rbufd, rd_sem, COLS, c) / D)
    rnd[...] = rn
    rroot = lax.rsqrt(rn)
    for a in range(8):
        rbd[a * 128 : a * 128 + 128, :] = jnp.transpose(
            jnp.broadcast_to(rroot[a : a + 1, :], (128, 128))
        )

    def down_raw(a, total):
        rows = pl.ds(pl.multiple_of(a * 128, 128), 128)
        for j in range(4):
            raw = gd[rows, j * 128 : j * 128 + 128] * rbd[rows, :] * crd[j : j + 1, :]
            total = total + jnp.sum((raw * raw).reshape(16, 8, 128), axis=0)
        return total

    td = lax.fori_loop(0, 8, down_raw, jnp.zeros((8, 128), F32))
    tp1[1:2, :] = jnp.sum(td, axis=0, keepdims=True)

    rn = keep * rsu[...] + take * (finish(rbufu, ru_sem, COLS, c) / FF)
    rnu[...] = rn
    rroot = lax.rsqrt(rn)
    for a in range(2):
        rbu[a * 128 : a * 128 + 128, :] = jnp.transpose(
            jnp.broadcast_to(rroot[a : a + 1, :], (128, 128))
        )
    cn = keep * csu[...] + take * (finish(cbufu2, cu2_sem, 4, p) / D)
    cnu[...] = cn
    cru[...] = lax.rsqrt(cn)

    def up_raw(j, total):
        cols = pl.ds(pl.multiple_of(j * 128, 128), 128)
        raw = gu[:, cols] * rbu[...] * cru[pl.ds(j, 1), :]
        return total + jnp.sum((raw * raw).reshape(32, 8, 128), axis=0)

    tu = lax.fori_loop(0, 16, up_raw, jnp.zeros((8, 128), F32))
    tp1[0:1, :] = jnp.sum(tu, axis=0, keepdims=True)

    place = y * 8 + x * 2 + core
    start(tp1, tbuf1, t1_sem, 32, place, in_plane)
    finish_sends(cpu, cu1_sem, 8)
    finish_sends(rpu, ru_sem, COLS)
    finish_sends(cpu2, cu2_sem, 4)
    finish_sends(rpd, rd_sem, COLS)
    finish_sends(cpd, cd_sem, ROWS)
    tp2[...] = finish(tbuf1, t1_sem, 32, place)
    start(tp2, tbuf2, t2_sem, 16, zh * 4 + p, in_z)
    finish_sends(tp1, t1_sem, 32)
    totals = finish(tbuf2, t2_sem, 16, zh * 4 + p)
    rms = jnp.sqrt(jnp.sum(totals, axis=1, keepdims=True) / (float(D) * float(FF)))
    scale = 1.0 / jnp.maximum(CLIP_FLOOR, rms)
    cru[...] = cru[...] * scale[0:1, :]
    crd[...] = crd[...] * scale[1:2, :]

    def up_write(j, carry):
        cols = pl.ds(pl.multiple_of(j * 128, 128), 128)
        uu[:, cols] = (gu[:, cols] * rbu[...] * cru[pl.ds(j, 1), :]).astype(BF16)
        return carry

    lax.fori_loop(0, 16, up_write, 0)

    def down_write(a, carry):
        rows = pl.ds(pl.multiple_of(a * 128, 128), 128)
        for j in range(4):
            cols = slice(j * 128, j * 128 + 128)
            ud[rows, cols] = (gd[rows, cols] * rbd[rows, :] * crd[j : j + 1, :]).astype(BF16)
        return carry

    lax.fori_loop(0, 8, down_write, 0)
    finish_sends(tp2, t2_sem, 16)


def write_out(*refs):
    ins, outs, sem = refs[:6], refs[6:12], refs[12]
    copies = [
        pltpu.make_async_copy(a, b, sem.at[i]) for i, (a, b) in enumerate(zip(ins, outs))
    ]
    for copy in copies:
        copy.start()
    for copy in copies:
        copy.wait()


SHAPES = (
    ((256, 2048), BF16),
    ((2, 128), F32),
    ((16, 128), F32),
    ((1024, 512), BF16),
    ((8, 128), F32),
    ((4, 128), F32),
)


def on_device(ai, h, ah, o, rsu, csu, rsd, csd):
    dma = pltpu.SemaphoreType.DMA
    any_ = pl.BlockSpec(memory_space=pl.ANY)
    vmem = pl.BlockSpec(memory_space=pltpu.VMEM)
    f32 = lambda *shape: pltpu.VMEM(shape, F32)
    bf16 = lambda *shape: pltpu.VMEM(shape, BF16)
    res = pl.pallas_call(
        kernel,
        out_shape=tuple(pltpu.VMEM(shape, dtype) for shape, dtype in SHAPES),
        in_specs=[any_] * 8,
        out_specs=[vmem] * 6,
        scratch_shapes=[
            bf16(NB, 64, 256), bf16(NB, 64, 1024), bf16(NB, 2, 32, 2048), bf16(NB, 2, 32, 512),
            f32(256, 2048), f32(1024, 512), f32(256, 128), f32(1024, 128),
            f32(2, 128), f32(16, 128), f32(8, 128), f32(4, 128), f32(16, 128), f32(4, 128),
            f32(2, 128), f32(16, 128), f32(16, 128), f32(8, 128), f32(4, 128),
            f32(COLS, 2, 128), f32(8, 16, 128), f32(4, 16, 128), f32(COLS, 8, 128), f32(ROWS, 4, 128),
            f32(2, 128), f32(32, 2, 128), f32(2, 128), f32(16, 2, 128),
            dma((NB,)), dma((NB, AHC)), dma((NB,)), dma((NB,)), dma((4,)), dma((4,)),
            dma((NSEND,)), dma((8,)),
            dma((2, COLS)), dma((2, ROWS)), dma((2, COLS)), dma((2, 8)), dma((2, 4)),
            dma((2, 32)), dma((2, 16)),
        ],
        compiler_params=pltpu.CompilerParams(
            collective_id=0, has_side_effects=True, vmem_limit_bytes=VMEM_MB * 1024 * 1024
        ),
        cost_estimate=pl.CostEstimate(
            flops=2 * 2 * 1024 * 256 * 2048, bytes_accessed=3 << 20, transcendentals=0
        ),
    )(ai, h, ah, o, rsu.reshape(2, 128), csu.reshape(16, 128), rsd.reshape(8, 128), csd.reshape(4, 128))
    uu, rnu, cnu, ud, rnd, cnd = pl.pallas_call(
        write_out,
        out_shape=tuple(pltpu.HBM(shape, dtype) for shape, dtype in SHAPES),
        in_specs=[vmem] * 6,
        out_specs=[pl.BlockSpec(memory_space=pltpu.HBM)] * 6,
        scratch_shapes=[dma((6,))],
        compiler_params=pltpu.CompilerParams(has_side_effects=True),
    )(*[pltpu.with_memory_space_constraint(t, pltpu.VMEM) for t in res])
    return (uu, rnu.reshape(256), cnu.reshape(2048), ud, rnd.reshape(1024), cnd.reshape(512))


def solution(mesh):
    in_specs = (
        P("col", "row"),
        P("row", "col"),
        P("col", "row"),
        P("row", "col"),
        P("row"),
        P("col"),
        P("row"),
        P("col"),
    )
    out_specs = (P("row", "col"), P("row"), P("col"), P("row", "col"), P("row"), P("col"))
    return jax.shard_map(
        on_device, mesh=mesh, in_specs=in_specs, out_specs=out_specs, check_vma=False
    )
```

time: 550 us -> 90.4 us (0.16)
  blocking collectives: 346 us -> 0 us
  waiting for transfers between devices: 172 us -> 0 us
  Pallas kernels: 0 us -> 89.7 us
  between operations: 15.3 us -> 0.64 us
  matrix products: 8.04 us -> 0 us
  other arithmetic: 7.39 us -> 0 us
    psum x3 -> x0, blocking collectives: 287 us -> none  [the longest x1 130 us: factored_update(): col_sum = lax.psum(col_part, 'row')]
    all_gather x3 -> x0, waiting for transfers between devices: 170 us -> none  [the longest x1 96.2 us: on_device(): lax.all_gather(acts_hidden, 'col', axis=0, tiled=True)]
    pallas_call x0 -> x2, Pallas kernels: none -> 89.7 us  [the longest x1 88.3 us: on_device(): pl.pallas_call(kernel, out_shape=tuple((pltpu.VMEM(shape, dtype) for shap...]
    all_gather x1 -> x0, blocking collectives: 59.1 us -> none  [on_device(): inputs_whole = lax.all_gather(acts_in, 'col', axis=0, tiled=True)]
    dot_general x2 -> x0, matrix products: 8.04 us -> none  [accumulate(): lax.dot_general(first, second, (((0,), (0,)), ((), ())), preferred_elemen...]
  transfers between devices with their start and end apart: 3 -> 0, of which waited for: 3 -> 0; matrix products, arithmetic and copies ran while one was open for 1% -> 0% of each run, Pallas kernels for 0% -> 0%
where the time goes in v2:
time: 90.4 us; the launch traced here: 90.3 us
  Pallas kernels  89.7 us (99%)
    pallas_call x1, Pallas kernels, on_device(): pl.pallas_call(kernel, out_shape=tuple((pltpu.VMEM(shape, dtype) for shap...  88.3 us

profile of v2, /device:TPU:1, one launch (start us, length us, event | category | flops | bytes accessed | tf_op | source)
XLA Modules:
  0.0 90.3 jit_solution(5908538755944845301)
XLA Ops:
  0.6 88.3 %shard_map.127 = (bf16[256,2048]{1,0:T(8,128)(2,1)S(1)}, f32[2,128]{1,0:T(2,128)S(1)}, f32[16,128]{1,0:T(8,128)S(1)}, bf16[1024,512]{1,0:T(8,128)(2,1)S(1)}, f32[8,128]{1,0:T(8,128)S(1)}, /*index=5*/f32[4,128]{1,0:T(4,128)S(1)}) custom-call(bf16[64,256]{1,0:T(8,128)(2,1)} %ai_in.1, bf16[32,2048]{1,0:T(8,128)(2,1)} %h_in.1, bf16[64,1024]{1,0:T(8,128)(2,1)} %ah_in.1, ...), custom_call_target="tpu_custom_call" | custom-call | flops 2147483648 | bytes 3145728 | tf_op jit(solution)/shard_map/pallas_call | solution.py:413
  88.9 1.4 %shard_map.128 = (bf16[256,2048]{1,0:T(8,128)(2,1)}, f32[2,128]{1,0:T(2,128)}, f32[16,128]{1,0:T(8,128)}, bf16[1024,512]{1,0:T(8,128)(2,1)}, f32[8,128]{1,0:T(8,128)}, /*index=5*/f32[4,128]{1,0:T(4,128)}) custom-call(bf16[256,2048]{1,0:T(8,128)(2,1)S(1)} %get-tuple-element.18.refs_0_, f32[2,128]{1,0:T(2,128)S(1)} %get-tuple-element.19.refs_1_, ...), custom_call_target="tpu_custom_call" | custom-call | tf_op jit(solution)/shard_map/pallas_call | solution.py:437

commit v3 on v2

--- a/solution.py
+++ b/solution.py
@@ -14,11 +14,12 @@
 NB = 16
 ROWS = 32
 COLS = 16
+HC = 1
 AHC = 2
 F32 = jnp.float32
 BF16 = jnp.bfloat16
 MESH = pl.DeviceIdType.MESH
-NSEND = 200
+NSEND = 240
 VMEM_MB = 57
 
 
@@ -30,9 +31,9 @@
     ai_in, h_in, ah_in, o_in, rsu_in, csu_in, rsd_in, csd_in,
     uu, rnu, cnu, ud, rnd, cnd,
     ai, ah, h, o, gu, gd, rbu, rbd, rsu, csu, rsd, csd, cru, crd,
-    rpu, cpu, cpu2, rpd, cpd, rbufu, cbufu, cbufu2, rbufd, cbufd, tp1, tbuf1, tp2, tbuf2,
+    rpu, cpu, cpu2, rpd, cpd, cpd2, rbufu, cbufu, cbufu2, rbufd, cbufd, cbufd2, tp1, tbuf1, tp2, tbuf2,
     ai_sem, ah_sem, h_sem, o_sem, hs_sem, os_sem, send_sem, loc_sem,
-    rd_sem, cd_sem, ru_sem, cu1_sem, cu2_sem, t1_sem, t2_sem,
+    rd_sem, cd1_sem, cd2_sem, ru_sem, cu1_sem, cu2_sem, t1_sem, t2_sem,
 ):
     r = lax.axis_index("row")
     c = lax.axis_index("col")
@@ -77,8 +78,15 @@
     def arrived(dst, recv, like=None):
         pltpu.make_async_remote_copy(dst, dst, send_sem.at[0], recv, sib, MESH).wait_recv()
 
-    def hslot(b):
-        return h.at[b, core], h_sem.at[b], lambda: h.at[0, 0]
+    HT = 32 // HC
+
+    def hslot(t):
+        part = pl.ds(t * HT, HT)
+
+        def slot(b):
+            return h.at[b, core, part], h_sem.at[b, t], lambda: h.at[0, 0, part]
+
+        return slot
 
     def oslot(b):
         return o.at[b, core], o_sem.at[b], lambda: o.at[0, 0]
@@ -98,6 +106,7 @@
 
     not_last, not_first = p < 3, p > 0
     own_r, own_c = p * 4 + x, c
+    h_own = [h_in.at[pl.ds(t * HT, HT)] for t in range(HC)]
     ah_own = [ah_in.at[pl.ds(t * AHT, AHT)] for t in range(AHC)]
 
     def line_own(src, slot):
@@ -113,10 +122,11 @@
         for dev in devs:
             send(src, *slot(b), dev, conds)
 
-    line_own(h_in, hslot)
+    line_own(h_own[0], hslot(0))
     spread(ah_own[0], ahslot(0), own_c, (z_f, z_b))
     line_own(o_in, oslot)
-    spread(h_in, hslot, own_r, xs)
+    for t in range(HC):
+        spread(h_own[t], hslot(t), own_r, xs)
     for t in range(AHC):
         spread(ah_own[t], ahslot(t), own_c, ys)
     spread(o_in, oslot, own_r, xs)
@@ -163,19 +173,16 @@
     def z_second(slot):
         z_one(slot, z2)
 
-    def to_sibling(d):
+    def to_sibling(buf, sem, slots, mine, d):
         def one(q, conds):
             for i in (1, 3, 2):
-                b = q * 4 + mod(x + i, 4)
-                arrived(*hslot(b))
-                arrived(*oslot(b))
-            for buf, sem in ((h, hs_sem), (o, os_sem)):
-                part = buf.at[pl.ds(q * 4, 4), core]
-                send(part, part, sem.at[q], lambda buf=buf: buf.at[pl.ds(0, 4), 0], sib, conds)
+                for slot in slots:
+                    arrived(*slot(q * 4 + mod(x + i, 4)))
+            part = buf.at[pl.ds(q * 4, 4), core]
+            send(part, part, sem.at[q], lambda: buf.at[pl.ds(0, 4), 0], sib, conds)
 
         if d == 0:
-            local[2].wait()
-            local[3].wait()
+            mine.wait()
             one(p, ())
         else:
             left, right = p >= d, p + d <= 3
@@ -186,74 +193,92 @@
         for i in (1, 3, 2):
             arrived(*slot(q * 4 + mod(y + i, 4)))
 
-    line(hslot, 1)
+    def product(a, b):
+        return lax.dot_general(a, b, (((0,), (0,)), ((), ())), preferred_element_type=F32)
+
+
+    def start(part, buf, sem, me, *groups):
+        for first, last, where in groups:
+
+            def one(k, carry, where=where):
+                pltpu.make_async_remote_copy(
+                    part, buf.at[me], sem.at[1], sem.at[0], where(k), MESH
+                ).start()
+                return carry
+
+            lax.fori_loop(first, last, one, 0)
+        buf[me] = part[...]
+
+    def finish(buf, sem, n):
+        others = buf.at[pl.ds(0, n - 1)]
+        pltpu.make_async_remote_copy(others, others, sem.at[1], sem.at[0], sib, MESH).wait_recv()
+        return jnp.sum(buf[...], axis=0)
+
+    def finish_sends(buf, sem, n):
+        others = buf.at[pl.ds(0, n - 1)]
+        pltpu.make_async_remote_copy(others, others, sem.at[1], sem.at[0], sib, MESH).wait_send()
+
+    on_x = x * 2 + core
+    in_x = ((1, 8, lambda k: (p * 8 + lax.rem(on_x + k, 8), c)),)
+    in_line = tuple((d, d + 1, lambda k: (lax.rem(p + k, 4) * 8 + on_x, c)) for d in (2, 1, 3))
+
+    def around(d, first, last, group, base):
+        at = group(d)
+        return (first, last, lambda k: base(at, k))
+
+    def col_of(d):
+        return around(d, 1 if d == 0 else 0, 4, lambda d: mod(zh + d, 4) * 4, lambda at, k: (r, at + lax.rem(y + k, 4)))
+
+    def plane_of(d):
+        return around(d, 1 if d == 0 else 0, 8, lambda d: zh * 4 + mod(y + d, 4), lambda at, k: (p * 8 + lax.rem(on_x + k, 8), at))
+
+    def z_of(d):
+        return around(d, 1 if d == 0 else 0, 4, lambda d: mod(zh + d, 4) * 4 + y, lambda at, k: (lax.rem(p + k, 4) * 8 + on_x, at))
+
+    in_col = [col_of(d) for d in (2, 1, 3, 0)]
+    in_plane = [plane_of(d) for d in (2, 1, 3, 0)]
+    in_z = [z_of(d) for d in (2, 1, 3, 0)]
+
+    def down_part(i):
+        q = (zh, zb, zf, z2)[i]
+        for t in range(AHC):
+            y_last(ahslot(t), q)
+        b = pl.ds(q * 4, 4)
+        term = product(ah[b].reshape(256, 1024), o[b].reshape(256, 512))
+        if i == 0:
+            gd[...] = term
+        else:
+            gd[...] += term
+
+    line(hslot(0), 1)
     z_first(ahslot(0))
     spread(ah_own[1], ahslot(1), own_c, (z_f, z_b))
     line(oslot, 1)
-    line(hslot, 2)
+    line(hslot(0), 2)
     z_first(ahslot(1))
     spread(ai_in, aislot, own_c, (z_f, z_b))
     line(oslot, 2)
     z_second(ahslot(0))
-    line(hslot, 3)
-    to_sibling(0)
+    line(hslot(0), 3)
+    to_sibling(o, os_sem, [oslot], local[3], 0)
+    to_sibling(h, hs_sem, [hslot(t) for t in range(HC)], local[2], 0)
     line(oslot, 3)
     z_first(aislot)
     z_second(ahslot(1))
-    to_sibling(1)
+    to_sibling(o, os_sem, [oslot], local[3], 1)
+    to_sibling(h, hs_sem, [hslot(t) for t in range(HC)], local[2], 1)
     z_second(aislot)
-    to_sibling(2)
-    to_sibling(3)
-    def product(a, b):
-        return lax.dot_general(a, b, (((0,), (0,)), ((), ())), preferred_element_type=F32)
-
-    def start(part, buf, sem, n, me, where):
-        def one(k, carry):
-            pltpu.make_async_remote_copy(
-                part, buf.at[me], sem.at[1, k], sem.at[0, me], where(mod(me + k, n)), MESH
-            ).start()
-            return carry
-
-        lax.fori_loop(1, n, one, 0)
-        buf[me] = part[...]
-
-    def finish(buf, sem, n, me):
-        def one(k, carry):
-            frm = mod(me + k, n)
-            pltpu.make_async_remote_copy(
-                buf.at[frm], buf.at[frm], sem.at[1, k], sem.at[0, frm], sib, MESH
-            ).wait_recv()
-            return carry
-
-        lax.fori_loop(1, n, one, 0)
-        return jnp.sum(buf[...], axis=0)
-
-    def finish_sends(part, sem, n):
-        def one(k, carry):
-            pltpu.make_async_remote_copy(
-                part, part, sem.at[1, k], sem.at[0, 0], sib, MESH
-            ).wait_send()
-            return carry
-
-        lax.fori_loop(1, n, one, 0)
-
-    to_row = lambda k: (k, c)
-    to_col = lambda k: (r, k)
-    in_x = lambda k: (p * 8 + k, c)
-    in_line = lambda k: (k * 8 + lax.rem(r, 8), c)
-    in_plane = lambda k: (p * 8 + lax.rem(k, 8), zh * 4 + k // 8)
-    in_z = lambda k: (lax.rem(k, 4) * 8 + lax.rem(r, 8), (k // 4) * 4 + y)
-
-
+    to_sibling(o, os_sem, [oslot], local[3], 2)
+    to_sibling(o, os_sem, [oslot], local[3], 3)
+    to_sibling(h, hs_sem, [hslot(t) for t in range(HC)], local[2], 2)
+    to_sibling(h, hs_sem, [hslot(t) for t in range(HC)], local[2], 3)
     local[1].wait()
     for q in range(4):
         arrived(o.at[pl.ds(q * 4, 4), 1 - core], os_sem.at[q])
-    for q in (zh, zb, zf, z2):
-        for t in range(AHC):
-            y_last(ahslot(t), q)
-    lhs_down = ah[...].reshape(1024, 1024)
-    gd[...] = product(lhs_down, o[...].reshape(1024, 512))
-
+    down_part(0)
+    down_part(1)
+    down_part(2)
+    down_part(3)
     ctotal = jnp.zeros((8, 512), F32)
     for a in range(8):
         g = gd[a * 128 : a * 128 + 128, :]
@@ -265,8 +290,8 @@
     for j in range(4):
         cpd[j : j + 1, :] = csum[:, j * 128 : j * 128 + 128]
 
-    start(rpd, rbufd, rd_sem, COLS, c, to_col)
-    start(cpd, cbufd, cd_sem, ROWS, r, to_row)
+    start(rpd, rbufd, rd_sem, c, *in_col)
+    start(cpd, cbufd, cd1_sem, on_x, *in_x)
 
     local[0].wait()
     for q in range(4):
@@ -296,11 +321,13 @@
         )
 
 
-    start(cpu, cbufu, cu1_sem, 8, x * 2 + core, in_x)
-    start(rpu, rbufu, ru_sem, COLS, c, to_col)
-
-    cpu2[...] = finish(cbufu, cu1_sem, 8, x * 2 + core)
-    start(cpu2, cbufu2, cu2_sem, 4, p, in_line)
+    start(cpu, cbufu, cu1_sem, on_x, *in_x)
+    start(rpu, rbufu, ru_sem, c, *in_col)
+
+    cpd2[...] = finish(cbufd, cd1_sem, 8)
+    start(cpd2, cbufd2, cd2_sem, p, *in_line)
+    cpu2[...] = finish(cbufu, cu1_sem, 8)
+    start(cpu2, cbufu2, cu2_sem, p, *in_line)
 
     for k, (like, conds) in enumerate(sends):
         when(conds, lambda: pltpu.make_async_remote_copy(
@@ -309,10 +336,10 @@
         copy.wait()
 
     keep, take = DECAY, 1.0 - DECAY
-    cn = keep * csd[...] + take * (finish(cbufd, cd_sem, ROWS, r) / FF)
+    cn = keep * csd[...] + take * (finish(cbufd2, cd2_sem, 4) / FF)
     cnd[...] = cn
     crd[...] = lax.rsqrt(cn)
-    rn = keep * rsd[...] + take * (finish(rbufd, rd_sem, COLS, c) / D)
+    rn = keep * rsd[...] + take * (finish(rbufd, rd_sem, COLS) / D)
     rnd[...] = rn
     rroot = lax.rsqrt(rn)
     for a in range(8):
@@ -323,64 +350,58 @@
     def down_raw(a, total):
         rows = pl.ds(pl.multiple_of(a * 128, 128), 128)
         for j in range(4):
-            raw = gd[rows, j * 128 : j * 128 + 128] * rbd[rows, :] * crd[j : j + 1, :]
+            cols = slice(j * 128, j * 128 + 128)
+            raw = gd[rows, cols] * rbd[rows, :] * crd[j : j + 1, :]
+            gd[rows, cols] = raw
             total = total + jnp.sum((raw * raw).reshape(16, 8, 128), axis=0)
         return total
 
     td = lax.fori_loop(0, 8, down_raw, jnp.zeros((8, 128), F32))
     tp1[1:2, :] = jnp.sum(td, axis=0, keepdims=True)
 
-    rn = keep * rsu[...] + take * (finish(rbufu, ru_sem, COLS, c) / FF)
+    rn = keep * rsu[...] + take * (finish(rbufu, ru_sem, COLS) / FF)
     rnu[...] = rn
     rroot = lax.rsqrt(rn)
     for a in range(2):
         rbu[a * 128 : a * 128 + 128, :] = jnp.transpose(
             jnp.broadcast_to(rroot[a : a + 1, :], (128, 128))
         )
-    cn = keep * csu[...] + take * (finish(cbufu2, cu2_sem, 4, p) / D)
+    cn = keep * csu[...] + take * (finish(cbufu2, cu2_sem, 4) / D)
     cnu[...] = cn
     cru[...] = lax.rsqrt(cn)
 
     def up_raw(j, total):
         cols = pl.ds(pl.multiple_of(j * 128, 128), 128)
         raw = gu[:, cols] * rbu[...] * cru[pl.ds(j, 1), :]
+        gu[:, cols] = raw
         return total + jnp.sum((raw * raw).reshape(32, 8, 128), axis=0)
 
     tu = lax.fori_loop(0, 16, up_raw, jnp.zeros((8, 128), F32))
     tp1[0:1, :] = jnp.sum(tu, axis=0, keepdims=True)
 
-    place = y * 8 + x * 2 + core
-    start(tp1, tbuf1, t1_sem, 32, place, in_plane)
-    finish_sends(cpu, cu1_sem, 8)
-    finish_sends(rpu, ru_sem, COLS)
-    finish_sends(cpu2, cu2_sem, 4)
-    finish_sends(rpd, rd_sem, COLS)
-    finish_sends(cpd, cd_sem, ROWS)
-    tp2[...] = finish(tbuf1, t1_sem, 32, place)
-    start(tp2, tbuf2, t2_sem, 16, zh * 4 + p, in_z)
-    finish_sends(tp1, t1_sem, 32)
-    totals = finish(tbuf2, t2_sem, 16, zh * 4 + p)
+    start(tp1, tbuf1, t1_sem, y * 8 + on_x, *in_plane)
+    finish_sends(cbufu, cu1_sem, 8)
+    finish_sends(rbufu, ru_sem, COLS)
+    finish_sends(cbufu2, cu2_sem, 4)
+    finish_sends(rbufd, rd_sem, COLS)
+    finish_sends(cbufd, cd1_sem, 8)
+    finish_sends(cbufd2, cd2_sem, 4)
+    tp2[...] = finish(tbuf1, t1_sem, 32)
+    start(tp2, tbuf2, t2_sem, zh * 4 + p, *in_z)
+    finish_sends(tbuf1, t1_sem, 32)
+    totals = finish(tbuf2, t2_sem, 16)
     rms = jnp.sqrt(jnp.sum(totals, axis=1, keepdims=True) / (float(D) * float(FF)))
     scale = 1.0 / jnp.maximum(CLIP_FLOOR, rms)
-    cru[...] = cru[...] * scale[0:1, :]
-    crd[...] = crd[...] * scale[1:2, :]
-
-    def up_write(j, carry):
-        cols = pl.ds(pl.multiple_of(j * 128, 128), 128)
-        uu[:, cols] = (gu[:, cols] * rbu[...] * cru[pl.ds(j, 1), :]).astype(BF16)
+
+    def write(i, carry):
+        rows = pl.ds(pl.multiple_of(i * 64, 64), 64)
+        uu[rows, :] = (gu[rows, :] * scale[0:1, :]).astype(BF16)
+        rows = pl.ds(pl.multiple_of(i * 256, 256), 256)
+        ud[rows, :] = (gd[rows, :] * scale[1:2, :]).astype(BF16)
         return carry
 
-    lax.fori_loop(0, 16, up_write, 0)
-
-    def down_write(a, carry):
-        rows = pl.ds(pl.multiple_of(a * 128, 128), 128)
-        for j in range(4):
-            cols = slice(j * 128, j * 128 + 128)
-            ud[rows, cols] = (gd[rows, cols] * rbd[rows, :] * crd[j : j + 1, :]).astype(BF16)
-        return carry
-
-    lax.fori_loop(0, 8, down_write, 0)
-    finish_sends(tp2, t2_sem, 16)
+    lax.fori_loop(0, 4, write, 0)
+    finish_sends(tbuf2, t2_sem, 16)
 
 
 def write_out(*refs):
@@ -419,13 +440,13 @@
             bf16(NB, 64, 256), bf16(NB, 64, 1024), bf16(NB, 2, 32, 2048), bf16(NB, 2, 32, 512),
             f32(256, 2048), f32(1024, 512), f32(256, 128), f32(1024, 128),
             f32(2, 128), f32(16, 128), f32(8, 128), f32(4, 128), f32(16, 128), f32(4, 128),
-            f32(2, 128), f32(16, 128), f32(16, 128), f32(8, 128), f32(4, 128),
-            f32(COLS, 2, 128), f32(8, 16, 128), f32(4, 16, 128), f32(COLS, 8, 128), f32(ROWS, 4, 128),
+            f32(2, 128), f32(16, 128), f32(16, 128), f32(8, 128), f32(4, 128), f32(4, 128),
+            f32(COLS, 2, 128), f32(8, 16, 128), f32(4, 16, 128), f32(COLS, 8, 128), f32(8, 4, 128), f32(4, 4, 128),
             f32(2, 128), f32(32, 2, 128), f32(2, 128), f32(16, 2, 128),
-            dma((NB,)), dma((NB, AHC)), dma((NB,)), dma((NB,)), dma((4,)), dma((4,)),
+            dma((NB,)), dma((NB, AHC)), dma((NB, HC)), dma((NB,)), dma((4,)), dma((4,)),
             dma((NSEND,)), dma((8,)),
-            dma((2, COLS)), dma((2, ROWS)), dma((2, COLS)), dma((2, 8)), dma((2, 4)),
-            dma((2, 32)), dma((2, 16)),
+            *[dma((2,))] * 6,
+            *[dma((2,))] * 2,
         ],
         compiler_params=pltpu.CompilerParams(
             collective_id=0, has_side_effects=True, vmem_limit_bytes=VMEM_MB * 1024 * 1024

time: 90.4 us -> 86.8 us (0.960)
  Pallas kernels: 89.7 us -> 86 us
    pallas_call x1, Pallas kernels: 88.3 us -> 84.6 us  [on_device(): pl.pallas_call(kernel, out_shape=tuple((pltpu.VMEM(shape, dtype) for shap...]
where the time goes in v3:
time: 86.8 us; the launch traced here: 86.6 us
  Pallas kernels  86 us (99%)
    pallas_call x1, Pallas kernels, on_device(): pl.pallas_call(kernel, out_shape=tuple((pltpu.VMEM(shape, dtype) for shap...  84.6 us

profile of v3, /device:TPU:1, one launch (start us, length us, event | category | flops | bytes accessed | tf_op | source)
XLA Modules:
  0.0 86.6 jit_solution(10871299084067325267)
XLA Ops:
  0.6 84.6 %shard_map.127 = (bf16[256,2048]{1,0:T(8,128)(2,1)S(1)}, f32[2,128]{1,0:T(2,128)S(1)}, f32[16,128]{1,0:T(8,128)S(1)}, bf16[1024,512]{1,0:T(8,128)(2,1)S(1)}, f32[8,128]{1,0:T(8,128)S(1)}, /*index=5*/f32[4,128]{1,0:T(4,128)S(1)}) custom-call(bf16[64,256]{1,0:T(8,128)(2,1)} %ai_in.1, bf16[32,2048]{1,0:T(8,128)(2,1)} %h_in.1, bf16[64,1024]{1,0:T(8,128)(2,1)} %ah_in.1, ...), custom_call_target="tpu_custom_call" | custom-call | flops 2147483648 | bytes 3145728 | tf_op jit(solution)/shard_map/pallas_call | solution.py:434
  85.3 1.4 %shard_map.128 = (bf16[256,2048]{1,0:T(8,128)(2,1)}, f32[2,128]{1,0:T(2,128)}, f32[16,128]{1,0:T(8,128)}, bf16[1024,512]{1,0:T(8,128)(2,1)}, f32[8,128]{1,0:T(8,128)}, /*index=5*/f32[4,128]{1,0:T(4,128)}) custom-call(bf16[256,2048]{1,0:T(8,128)(2,1)S(1)} %get-tuple-element.18.refs_0_, f32[2,128]{1,0:T(2,128)S(1)} %get-tuple-element.19.refs_1_, ...), custom_call_target="tpu_custom_call" | custom-call | tf_op jit(solution)/shard_map/pallas_call | solution.py:458

commit v4 on v3

--- a/solution.py
+++ b/solution.py
@@ -123,14 +123,15 @@
             send(src, *slot(b), dev, conds)
 
     line_own(h_own[0], hslot(0))
+    spread(ai_in, aislot, own_c, (z_f, z_b))
     spread(ah_own[0], ahslot(0), own_c, (z_f, z_b))
     line_own(o_in, oslot)
     for t in range(HC):
         spread(h_own[t], hslot(t), own_r, xs)
+    spread(ai_in, aislot, own_c, ys)
     for t in range(AHC):
         spread(ah_own[t], ahslot(t), own_c, ys)
     spread(o_in, oslot, own_r, xs)
-    spread(ai_in, aislot, own_c, ys)
 
     local = [
         pltpu.make_async_copy(ai_in, ai.at[own_c], loc_sem.at[0]),
@@ -251,27 +252,57 @@
             gd[...] += term
 
     line(hslot(0), 1)
+    z_first(aislot)
     z_first(ahslot(0))
     spread(ah_own[1], ahslot(1), own_c, (z_f, z_b))
     line(oslot, 1)
     line(hslot(0), 2)
+    z_second(aislot)
     z_first(ahslot(1))
-    spread(ai_in, aislot, own_c, (z_f, z_b))
     line(oslot, 2)
     z_second(ahslot(0))
     line(hslot(0), 3)
     to_sibling(o, os_sem, [oslot], local[3], 0)
     to_sibling(h, hs_sem, [hslot(t) for t in range(HC)], local[2], 0)
     line(oslot, 3)
-    z_first(aislot)
     z_second(ahslot(1))
     to_sibling(o, os_sem, [oslot], local[3], 1)
     to_sibling(h, hs_sem, [hslot(t) for t in range(HC)], local[2], 1)
-    z_second(aislot)
     to_sibling(o, os_sem, [oslot], local[3], 2)
     to_sibling(o, os_sem, [oslot], local[3], 3)
     to_sibling(h, hs_sem, [hslot(t) for t in range(HC)], local[2], 2)
     to_sibling(h, hs_sem, [hslot(t) for t in range(HC)], local[2], 3)
+
+    local[0].wait()
+    for q in range(4):
+        arrived(h.at[pl.ds(q * 4, 4), 1 - core], hs_sem.at[q])
+    for q in (zh, zb, zf, z2):
+        y_last(aislot, q)
+    lhs = ai[...].reshape(1024, 256)
+
+    def up_tile(n, carry):
+        cols = pl.ds(pl.multiple_of(n * 512, 512), 512)
+        gu[:, cols] = product(lhs, h[:, :, :, cols].reshape(1024, 512))
+        return carry
+
+    lax.fori_loop(0, 4, up_tile, 0)
+
+    def up_squares(j, sums):
+        cols = pl.ds(pl.multiple_of(j * 128, 128), 128)
+        g = gu[:, cols]
+        sq = g * g + EPS_SQUARE
+        cpu[pl.ds(j, 1), :] = jnp.sum(sq, axis=0, keepdims=True)
+        return sums + sq
+
+    sums = lax.fori_loop(0, 16, up_squares, jnp.zeros((256, 128), F32))
+    for a in range(2):
+        rpu[a : a + 1, :] = jnp.sum(
+            jnp.transpose(sums[a * 128 : a * 128 + 128]), axis=0, keepdims=True
+        )
+
+
+    start(cpu, cbufu, cu1_sem, on_x, *in_x)
+    start(rpu, rbufu, ru_sem, c, *in_col)
     local[1].wait()
     for q in range(4):
         arrived(o.at[pl.ds(q * 4, 4), 1 - core], os_sem.at[q])
@@ -292,37 +323,6 @@
 
     start(rpd, rbufd, rd_sem, c, *in_col)
     start(cpd, cbufd, cd1_sem, on_x, *in_x)
-
-    local[0].wait()
-    for q in range(4):
-        arrived(h.at[pl.ds(q * 4, 4), 1 - core], hs_sem.at[q])
-    for q in (zh, zb, zf, z2):
-        y_last(aislot, q)
-    lhs = ai[...].reshape(1024, 256)
-
-    def up_tile(n, carry):
-        cols = pl.ds(pl.multiple_of(n * 512, 512), 512)
-        gu[:, cols] = product(lhs, h[:, :, :, cols].reshape(1024, 512))
-        return carry
-
-    lax.fori_loop(0, 4, up_tile, 0)
-
-    def up_squares(j, sums):
-        cols = pl.ds(pl.multiple_of(j * 128, 128), 128)
-        g = gu[:, cols]
-        sq = g * g + EPS_SQUARE
-        cpu[pl.ds(j, 1), :] = jnp.sum(sq, axis=0, keepdims=True)
-        return sums + sq
-
-    sums = lax.fori_loop(0, 16, up_squares, jnp.zeros((256, 128), F32))
-    for a in range(2):
-        rpu[a : a + 1, :] = jnp.sum(
-            jnp.transpose(sums[a * 128 : a * 128 + 128]), axis=0, keepdims=True
-        )
-
-
-    start(cpu, cbufu, cu1_sem, on_x, *in_x)
-    start(rpu, rbufu, ru_sem, c, *in_col)
 
     cpd2[...] = finish(cbufd, cd1_sem, 8)
     start(cpd2, cbufd2, cd2_sem, p, *in_line)

time: 86.8 us -> 88.8 us (1.023)
  Pallas kernels: 86 us -> 88.1 us
    pallas_call x1, Pallas kernels: 84.6 us -> 86.7 us  [on_device(): pl.pallas_call(kernel, out_shape=tuple((pltpu.VMEM(shape, dtype) for shap...]
where the time goes in v4:
time: 88.8 us; the launch traced here: 88.7 us
  Pallas kernels  88.1 us (99%)
    pallas_call x1, Pallas kernels, on_device(): pl.pallas_call(kernel, out_shape=tuple((pltpu.VMEM(shape, dtype) for shap...  86.7 us

profile of v4, /device:TPU:1, one launch (start us, length us, event | category | flops | bytes accessed | tf_op | source)
XLA Modules:
  0.0 88.7 jit_solution(18180268816548545499)
XLA Ops:
  0.6 86.7 %shard_map.127 = (bf16[256,2048]{1,0:T(8,128)(2,1)S(1)}, f32[2,128]{1,0:T(2,128)S(1)}, f32[16,128]{1,0:T(8,128)S(1)}, bf16[1024,512]{1,0:T(8,128)(2,1)S(1)}, f32[8,128]{1,0:T(8,128)S(1)}, /*index=5*/f32[4,128]{1,0:T(4,128)S(1)}) custom-call(bf16[64,256]{1,0:T(8,128)(2,1)} %ai_in.1, bf16[32,2048]{1,0:T(8,128)(2,1)} %h_in.1, bf16[64,1024]{1,0:T(8,128)(2,1)} %ah_in.1, ...), custom_call_target="tpu_custom_call" | custom-call | flops 2147483648 | bytes 3145728 | tf_op jit(solution)/shard_map/pallas_call | solution.py:434
  87.3 1.4 %shard_map.128 = (bf16[256,2048]{1,0:T(8,128)(2,1)}, f32[2,128]{1,0:T(2,128)}, f32[16,128]{1,0:T(8,128)}, bf16[1024,512]{1,0:T(8,128)(2,1)}, f32[8,128]{1,0:T(8,128)}, /*index=5*/f32[4,128]{1,0:T(4,128)}) custom-call(bf16[256,2048]{1,0:T(8,128)(2,1)S(1)} %get-tuple-element.18.refs_0_, f32[2,128]{1,0:T(2,128)S(1)} %get-tuple-element.19.refs_1_, ...), custom_call_target="tpu_custom_call" | custom-call | tf_op jit(solution)/shard_map/pallas_call | solution.py:458
